TPU v7x, 256 devices: a whole 4x4x8 slice. The times are simulated.
256 devices in a mesh: ent: 32 (over y, x, core), rel: 8 (over z).
Axes of the slice: x: 4, y: 4, z: 8, core: 2. Of those that a mesh axis runs over, the one named last changes fastest.
Arguments:
- tile_vals: bfloat16 [32, 8, 64, 128, 128], P('ent', 'rel'), may hold values from -192 to 192
- tile_row: int32 [32, 8, 64], P('ent', 'rel'), may hold values from 0 to 3
- tile_rel: int32 [32, 8, 64], P('ent', 'rel'), may hold values from 0 to 1
- tile_src: int32 [32, 8, 64], P('ent', 'rel'), may hold values from 0 to 31
- needed: int32 [32, 8, 32, 1], P('ent', 'rel'), may hold values from 0 to 3
- factors: bfloat16 [16384, 256], P('ent'), may hold values from -6 to 6
- cores: bfloat16 [16, 256, 256], P('rel'), may hold values from -0.5 to 1.5
- basis: float32 [256, 256], replicated, may hold values from -1 to 1
- spectrum: float32 [256], replicated, may hold values from 100 to 1000
Outputs:
- new_factors: bfloat16 [16384, 256], P('ent')
- new_cores: float32 [16, 256, 256], P('rel')
Inputs may be any that keep to these rules, and one draw needn't show every extreme that they name: tile_src names the owner whose single requested block (slot 0 of `needed`) gives the tile's columns. `needed`: every request slot names a block.
All inputs are finite; a program needn't handle non-finite values.
Results may differ from a plain program's by a relative error of at most 0.0081.
Values may be sent and summed in bfloat16 or wider, within the bound.
A program may use at most 64 MiB of HBM per device.

v0:
```python
import jax
import jax.numpy as jnp
from jax import lax
from jax.sharding import PartitionSpec as P

ridge_shift = 1.0


def shards(tile_vals, tile_row, tile_rel, tile_src, needed, factors, cores, basis, spectrum):
    precise = lax.Precision.HIGHEST
    tile_data = tile_vals[0, 0]
    tile_rows = tile_row[0, 0]
    tile_rels = tile_rel[0, 0]
    sources = tile_src[0, 0]
    asked_rows = needed[0, 0]
    count_ent, slot_count = asked_rows.shape
    tile_edge = tile_data.shape[1]
    rank_width = factors.shape[1]
    rel_local = cores.shape[0]
    row_blocks = factors.shape[0] // tile_edge
    slot_total = count_ent * slot_count
    requests = lax.all_to_all(asked_rows, "ent", split_axis=0, concat_axis=0, tiled=True)

    def neighbour(slab_rows):
        whole_table = lax.all_gather(slab_rows, "ent", axis=0, tiled=True).reshape(
            count_ent, row_blocks, tile_edge, rank_width
        )
        fetched = whole_table[jnp.arange(count_ent)[:, None], asked_rows]
        return fetched.reshape(slot_total, tile_edge, rank_width)[sources]

    def grouped(part_data, key_ids, group_count):
        onehot = (key_ids[:, None] == jnp.arange(group_count, dtype=jnp.int32)[None, :]).astype(
            jnp.bfloat16
        )
        flat_part = part_data.reshape(part_data.shape[0], tile_edge * rank_width)
        return jnp.einsum(
            "tg,tx->gx", onehot, flat_part, preferred_element_type=jnp.float32
        ).astype(jnp.bfloat16)

    gathered_old = neighbour(factors)
    left_part = jnp.einsum(
        "tab,tbr->tar", tile_data, gathered_old, preferred_element_type=jnp.float32
    ).astype(jnp.bfloat16)
    forward = grouped(
        left_part, tile_rels * row_blocks + tile_rows, rel_local * row_blocks
    ).reshape(rel_local, row_blocks, tile_edge, rank_width)
    forward_term = jnp.einsum(
        "kbar,ksr->bas", forward, cores, preferred_element_type=jnp.float32
    ).reshape(-1, rank_width)
    own_blocks = factors.reshape(row_blocks, tile_edge, rank_width)
    right_part = jnp.einsum(
        "tab,tar->tbr", tile_data, own_blocks[tile_rows], preferred_element_type=jnp.float32
    ).astype(jnp.bfloat16)
    backward = grouped(right_part, sources * rel_local + tile_rels, slot_total * rel_local).reshape(
        slot_total, rel_local, tile_edge, rank_width
    )
    backward_term = jnp.einsum(
        "skbr,krq->sbq", backward, cores, preferred_element_type=jnp.float32
    ).reshape(count_ent, slot_count, tile_edge, rank_width)
    returned = lax.all_to_all(backward_term, "ent", split_axis=0, concat_axis=0, tiled=True)
    landing = (
        requests.reshape(1, slot_total) == jnp.arange(row_blocks, dtype=jnp.int32)[:, None]
    ).astype(jnp.float32)
    landed = jnp.dot(
        landing,
        returned.reshape(slot_total, tile_edge * rank_width),
        precision=precise,
        preferred_element_type=jnp.float32,
    ).reshape(-1, rank_width)
    gram_total = lax.psum(
        jnp.einsum("ar,as->rs", factors, factors, preferred_element_type=jnp.float32), "ent"
    )
    core_f32 = cores.astype(jnp.float32)
    system_part = jnp.einsum("kab,bc,kdc->ad", core_f32, gram_total, core_f32, precision=precise)
    system_part = system_part + jnp.einsum(
        "kba,bc,kcd->ad", core_f32, gram_total, core_f32, precision=precise
    )
    numerator, system = lax.psum((forward_term + landed, system_part), "rel")
    system = system + ridge_shift * jnp.eye(rank_width, dtype=jnp.float32)
    factor_low = jnp.linalg.cholesky(system)
    new_factors = jax.scipy.linalg.cho_solve((factor_low, True), numerator.T).T.astype(jnp.bfloat16)
    gathered_new = neighbour(new_factors)
    latest = jnp.einsum(
        "tab,tbr->tar", tile_data, gathered_new, preferred_element_type=jnp.float32
    ).astype(jnp.bfloat16)
    summed = grouped(latest, tile_rels * row_blocks + tile_rows, rel_local * row_blocks).reshape(
        rel_local, row_blocks, tile_edge, rank_width
    )
    core_part = jnp.einsum(
        "bar,kbas->krs",
        new_factors.reshape(row_blocks, tile_edge, rank_width),
        summed,
        preferred_element_type=jnp.float32,
    )
    weights = 1.0 / (spectrum[:, None] * spectrum[None, :] + ridge_shift)
    totals = lax.psum(core_part, "ent")
    rotated = jnp.einsum("ri,krs,sj->kij", basis, totals, basis, precision=precise)
    new_cores = jnp.einsum(
        "ir,krs,js->kij", basis, weights[None] * rotated, basis, precision=precise
    )
    return (new_factors, new_cores)


def solution(mesh):
    in_specs = (
        P("ent", "rel", None, None, None),
        P("ent", "rel", None),
        P("ent", "rel", None),
        P("ent", "rel", None),
        P("ent", "rel", None, None),
        P("ent", None),
        P("rel", None, None),
        P(),
        P(),
    )
    out_specs = (P("ent", None), P("rel", None, None))
    return jax.shard_map(shards, mesh=mesh, in_specs=in_specs, out_specs=out_specs, check_vma=False)
```

profile of v0, /device:TPU:1, one launch (start us, length us, event | category | flops | bytes accessed | tf_op | source)
XLA Modules:
  0.0 606.0 jit_solution(6752421999504624473)
XLA Ops:
  11.5 8.6 %all-to-all-start = ((s32[32,1,1]{2,1,0:T(1,128)}), s32[32,1,1]{2,1,0:T(1,128)S(1)}, u32[]{:S(2)}, u32[]{:S(2)}) async-start(s32[32,1,1]{2,1,0:T(1,128)} %copy.58), calls=%async_computation | async-start | bytes 32768 | tf_op jit(solution)/shard_map/all_to_all | solution.py:22
  23.5 5.5 convert_bitcast_fusion.1
  29.0 6.8 %copy.96 = bf16[8,8,128,256]{3,1,2,0:T(8,128)(2,1)} copy(bf16[8,8,128,256]{2,3,1,0:T(8,128)(2,1)} %bitcast.176) | data formatting | bytes 8388608
  43.8 7.6 %all-to-all-start.1 = ((f32[32,1,128,256]{3,2,1,0:T(8,128)}), f32[32,1,128,256]{3,2,1,0:T(8,128)}, u32[]{:S(2)}, u32[]{:S(2)}) async-start(f32[32,1,128,256]{3,2,1,0:T(8,128)} %convolution_bitcast_fusion), calls=%async_computation.1 | async-start | bytes 8388608 | tf_op jit(solution)/shard_map/all_to_all | solution.py:60
  52.6 100.5 %all-reduce.6.cloned.1.call-done = f32[256,256]{1,0:T(8,128)} async-done(((f32[256,256]{1,0:T(8,128)}), f32[256,256]{1,0:T(8,128)}) %all-reduce.6.cloned.1.call-update) | async-done | bytes 262160 | tf_op jit(solution)/shard_map/psum | solution.py:70
  157.5 4.6 copy.98
  164.1 50.2 %all-gather.3.cloned.1.call-done = bf16[16384,256]{1,0:T(8,128)(2,1)} async-done(((bf16[512,256]{1,0:T(8,128)(2,1)}), bf16[16384,256]{1,0:T(8,128)(2,1)}) %all-gather.3.cloned.1.call-update) | async-done | bytes 8388624 | tf_op jit(solution)/shard_map/all_gather | solution.py:25
  214.2 5.4 gather_fusion
  219.7 4.4 gather_fusion.1
  224.0 5.5 convert_bitcast_fusion.2
  229.5 6.8 %copy.94 = bf16[8,8,128,256]{3,1,2,0:T(8,128)(2,1)} copy(bf16[8,8,128,256]{2,3,1,0:T(8,128)(2,1)} %bitcast.177) | data formatting | bytes 8388608
  240.8 69.7 %all-reduce.10.cloned.1.call-done = (f32[256,512]{0,1:T(8,128)}, f32[256,256]{0,1:T(8,128)}) async-done(((f32[256,512]{0,1:T(8,128)}, f32[256,256]{0,1:T(8,128)}), (f32[256,512]{0,1:T(8,128)}, f32[256,256]{0,1:T(8,128)})) %all-reduce.10.cloned.1.call-update) | async-done | bytes 786448 | tf_op jit(solution)/shard_map/psum | solution.py:78
  312.7 11.7 %cholesky.50 = f32[128,128]{1,0:T(8,128)S(1)} custom-call(f32[128,128]{1,0:T(8,128)S(1)} %cholesky.118), custom_call_target="Cholesky" | custom-call | tf_op jit(solution)/shard_map/jit(cholesky)/cholesky | solution.py:80
  324.4 9.8 %custom-call.18 = f32[1,128,128]{1,2,0:T(8,128)S(1)} custom-call(f32[1,128,128]{2,1,0:T(8,128)S(1)} %get-tuple-element.33), custom_call_target="InvertDiagBlocksLowerTriangular" | custom-call | tf_op jit(solution)/shard_map/jit(cholesky)/cholesky | solution.py:80
  334.7 11.7 %cholesky.105 = f32[128,128]{1,0:T(8,128)S(1)} custom-call(f32[128,128]{1,0:T(8,128)S(1)} %convolution_subtract_fusion.2), custom_call_target="Cholesky" | custom-call | tf_op jit(solution)/shard_map/jit(cholesky)/cholesky | solution.py:80
  348.5 4.2 while.1
  352.7 19.7 %custom-call.19 = f32[2,128,128]{1,2,0:T(8,128)S(1)} custom-call(f32[2,128,128]{2,1,0:T(8,128)S(1)} %get-tuple-element.9), custom_call_target="InvertDiagBlocksLowerTriangular" | custom-call | tf_op jit(solution)/shard_map/jit(_cho_solve)/triangular_solve | solution.py:81
  376.9 66.5 %all-gather.5.cloned.1.call-done = bf16[16384,256]{0,1:T(8,128)(2,1)} async-done(((bf16[512,256]{0,1:T(8,128)(2,1)}), bf16[16384,256]{0,1:T(8,128)(2,1)}) %all-gather.5.cloned.1.call-update) | async-done | bytes 8388624 | tf_op jit(solution)/shard_map/all_gather | solution.py:25
  443.4 12.0 %copy.92 = bf16[16384,256]{1,0:T(8,128)(2,1)} copy(bf16[16384,256]{0,1:T(8,128)(2,1)} %all-gather.5.cloned.1.call-done) | data formatting | bytes 16777216 | tf_op jit(solution)/shard_map/reshape | solution.py:25
  455.4 5.4 gather_fusion.3
  460.8 4.4 gather_fusion.4
  465.2 5.5 convert_bitcast_fusion
  470.7 6.8 %copy.99 = bf16[8,8,128,256]{3,1,2,0:T(8,128)(2,1)} copy(bf16[8,8,128,256]{2,3,1,0:T(8,128)(2,1)} %bitcast.178) | data formatting | bytes 8388608
  481.9 112.9 %all-reduce.8.cloned.1.call-done = f32[2,256,256]{1,2,0:T(8,128)} async-done(((f32[2,256,256]{1,2,0:T(8,128)}), f32[2,256,256]{1,2,0:T(8,128)}) %all-reduce.8.cloned.1.call-update) | async-done | bytes 524304 | tf_op jit(solution)/shard_map/psum | solution.py:96
  (95 shorter events, 48.1 us)
Async XLA Ops:
  7.2 16.4 %copy-start = (bf16[1,1,64,128,128]{4,3,2,1,0:T(8,128)(2,1)S(1)}, bf16[1,1,64,128,128]{4,3,2,1,0:T(8,128)(2,1)}, u32[]{:S(2)}) copy-start(bf16[1,1,64,128,128]{4,3,2,1,0:T(8,128)(2,1)} %param.9) | copy-start | bytes 6291460
  7.2 13.6 %copy-start.1 = (bf16[512,256]{1,0:T(8,128)(2,1)S(1)}, bf16[512,256]{1,0:T(8,128)(2,1)}, u32[]{:S(2)}) copy-start(bf16[512,256]{1,0:T(8,128)(2,1)} %param.14) | copy-start | bytes 786436
  7.2 145.9 %all-reduce.6.cloned.1.call-start = ((), (), s32[]{:S(2)}) async-start(), calls=%async_computation.2 | async-start | bytes 524288 | tf_op jit(solution)/shard_map/psum | solution.py:70
  9.4 204.8 %all-gather.3.cloned.1.call-start = ((), (), s32[]{:S(2)}) async-start(), calls=%async_computation.3 | async-start | bytes 8650752 | tf_op jit(solution)/shard_map/all_gather | solution.py:25
  11.5 32.2 %all-to-all-start = ((s32[32,1,1]{2,1,0:T(1,128)}), s32[32,1,1]{2,1,0:T(1,128)S(1)}, u32[]{:S(2)}, u32[]{:S(2)}) async-start(s32[32,1,1]{2,1,0:T(1,128)} %copy.58), calls=%async_computation | async-start | bytes 32768 | tf_op jit(solution)/shard_map/all_to_all | solution.py:22
  29.0 6.8 %copy-start.7 = (s32[1,1,64]{2,1,0:T(1,128)S(1)}, s32[1,1,64]{2,1,0:T(1,128)}, u32[]{:S(2)}) copy-start(s32[1,1,64]{2,1,0:T(1,128)} %param.10) | copy-start | bytes 772
  29.0 6.8 %copy-start.8 = (s32[1,1,64]{2,1,0:T(1,128)S(1)}, s32[1,1,64]{2,1,0:T(1,128)}, u32[]{:S(2)}) copy-start(s32[1,1,64]{2,1,0:T(1,128)} %param.11) | copy-start | bytes 772
  29.0 6.8 %copy-start.10 = (s32[1,1,64]{2,1,0:T(1,128)S(1)}, s32[1,1,64]{2,1,0:T(1,128)}, u32[]{:S(2)}) copy-start(s32[1,1,64]{2,1,0:T(1,128)} %param.12) | copy-start | bytes 772
  39.4 1.1 copy-start.2
  43.8 8.1 %copy-start.9 = (s32[1,1,32,1]{2,3,1,0:T(1,128)S(1)}, s32[1,1,32,1]{2,3,1,0:T(1,128)}, u32[]{:S(2)}) copy-start(s32[1,1,32,1]{2,3,1,0:T(1,128)} %param.13) | copy-start | bytes 388
  43.8 113.8 %all-to-all-start.1 = ((f32[32,1,128,256]{3,2,1,0:T(8,128)}), f32[32,1,128,256]{3,2,1,0:T(8,128)}, u32[]{:S(2)}, u32[]{:S(2)}) async-start(f32[32,1,128,256]{3,2,1,0:T(8,128)} %convolution_bitcast_fusion), calls=%async_computation.1 | async-start | bytes 8388608 | tf_op jit(solution)/shard_map/all_to_all | solution.py:60
  51.3 259.1 %all-reduce.10.cloned.1.call-start = ((), (), s32[]{:S(2)}) async-start(), calls=%async_computation.6 | async-start | bytes 1572864 | tf_op jit(solution)/shard_map/psum | solution.py:78
  240.5 202.9 %all-gather.5.cloned.1.call-start = ((), (), s32[]{:S(2)}) async-start(), calls=%async_computation.4 | async-start | bytes 8650752 | tf_op jit(solution)/shard_map/all_gather | solution.py:25
  310.5 61.9 %copy-start.5 = (f32[256,512]{0,1:T(8,128)S(1)}, f32[256,512]{0,1:T(8,128)}, u32[]{:S(2)}) copy-start(f32[256,512]{0,1:T(8,128)} %get-tuple-element.26) | copy-start | bytes 1572868
  375.8 219.1 %all-reduce.8.cloned.1.call-start = ((), (), s32[]{:S(2)}) async-start(), calls=%async_computation.5 | async-start | bytes 1048576 | tf_op jit(solution)/shard_map/psum | solution.py:96
  376.9 103.7 %copy-start.4 = (bf16[512,256]{1,0:T(8,128)(2,1)}, bf16[512,256]{1,0:T(8,128)(2,1)S(1)}, u32[]{:S(2)}) copy-start(bf16[512,256]{1,0:T(8,128)(2,1)S(1)} %copy.71) | copy-start | bytes 786436
  477.5 4.3 copy-start.6
  477.5 117.4 %copy-start.3 = (f32[256,256]{1,0:T(8,128)S(1)}, f32[256,256]{1,0:T(8,128)}, u32[]{:S(2)}) copy-start(f32[256,256]{1,0:T(8,128)} %param.16) | copy-start | bytes 786436
Sparse Core Ops, SparseCore 0:
  11.8 141.2 all-reduce.5
  156.0 58.1 all-gather.2
  240.7 69.7 all-reduce.9
  375.9 67.4 all-gather.4
  481.9 112.9 all-reduce.7
where the time goes:
time: 613 us; the launch traced here: 606 us
  waiting for transfers between devices  401 us (65%)
  local copies, waits for them, and re-layouts  67.8 us (11%)
  other arithmetic  57.9 us (9%)
  matrix products  46.8 us (8%)
  starting transfers between devices  17 us (3%)
  between operations  15.7 us (3%)
    all_gather x2, waiting for transfers between devices, neighbour(): lax.all_gather(slab_rows, 'ent', axis=0, tiled=True)  117 us
    psum x1, waiting for transfers between devices, shards(): totals = lax.psum(core_part, 'ent')  113 us
    psum x1, waiting for transfers between devices, shards(): lax.psum(jnp.einsum('ar,as->rs', factors, factors, preferred_element_type...  101 us
    psum x1, waiting for transfers between devices, shards(): numerator, system = lax.psum((forward_term + landed, system_part), 'rel')  69.7 us
    another operation x6, other arithmetic, shards(): factor_low = jnp.linalg.cholesky(system)  34 us
    unnamed x30, local copies, waits for them, and re-layouts  27.6 us
    another operation x3, other arithmetic, shards(): jax.scipy.linalg.cho_solve((factor_low, True), numerator.T)  19.7 us
  transfers between devices with their start and end apart: 7, of which 5 were waited for; matrix products, arithmetic and copies ran while one was open for 6% of the time, Pallas kernels for 0%

commit v1 on v0

--- a/solution.py
+++ b/solution.py
@@ -1,9 +1,18 @@
+import functools
 import jax
 import jax.numpy as jnp
 from jax import lax
 from jax.sharding import PartitionSpec as P
 
 ridge_shift = 1.0
+
+
+def _treat_bands(local_x, chip_axis):
+    later = lax.all_gather(local_x, chip_axis).sum(axis=0)
+    return later
+
+
+check_the_groups = functools.partial(_treat_bands, chip_axis="ent")
 
 
 def shards(tile_vals, tile_row, tile_rel, tile_src, needed, factors, cores, basis, spectrum):
@@ -67,8 +76,8 @@
         precision=precise,
         preferred_element_type=jnp.float32,
     ).reshape(-1, rank_width)
-    gram_total = lax.psum(
-        jnp.einsum("ar,as->rs", factors, factors, preferred_element_type=jnp.float32), "ent"
+    gram_total = check_the_groups(
+        jnp.einsum("ar,as->rs", factors, factors, preferred_element_type=jnp.float32)
     )
     core_f32 = cores.astype(jnp.float32)
     system_part = jnp.einsum("kab,bc,kdc->ad", core_f32, gram_total, core_f32, precision=precise)

time: 613 us -> 578 us (0.943)
  waiting for transfers between devices: 401 us -> 360 us
    psum x1 -> x0, waiting for transfers between devices: 101 us -> none  [shards(): lax.psum(jnp.einsum('ar,as->rs', factors, factors, preferred_element_type...]
    all_to_all x1, waiting for transfers between devices: 0.01 us -> 63.9 us  [shards(): lax.all_to_all(backward_term, 'ent', split_axis=0, concat_axis=0, tiled=T...]
    unnamed x30 -> x34, local copies, waits for them, and re-layouts: 27.6 us -> 27.5 us
  transfers between devices with their start and end apart: 7 -> 7, of which waited for: 5 -> 5; matrix products, arithmetic and copies ran while one was open for 6% -> 7% of each run, Pallas kernels for 0% -> 0%
where the time goes in v1:
time: 578 us; the launch traced here: 571 us
  waiting for transfers between devices  360 us (62%)
  local copies, waits for them, and re-layouts  68.9 us (12%)
  other arithmetic  61.8 us (11%)
  matrix products  47.5 us (8%)
  starting transfers between devices  17 us (3%)
  between operations  15.7 us (3%)
    all_gather x2, waiting for transfers between devices, neighbour(): lax.all_gather(slab_rows, 'ent', axis=0, tiled=True)  113 us
    psum x1, waiting for transfers between devices, shards(): totals = lax.psum(core_part, 'ent')  113 us
    psum x1, waiting for transfers between devices, shards(): numerator, system = lax.psum((forward_term + landed, system_part), 'rel')  69.7 us
    all_to_all x1, waiting for transfers between devices, shards(): lax.all_to_all(backward_term, 'ent', split_axis=0, concat_axis=0, tiled=T...  63.9 us
    another operation x6, other arithmetic, shards(): factor_low = jnp.linalg.cholesky(system)  33.9 us
    unnamed x34, local copies, waits for them, and re-layouts  27.5 us
    another operation x3, other arithmetic, shards(): jax.scipy.linalg.cho_solve((factor_low, True), numerator.T)  19.7 us
    reshape x1, local copies, waits for them, and re-layouts, neighbour(): lax.all_gather(slab_rows, 'ent', axis=0, tiled=True)  12 us
  transfers between devices with their start and end apart: 7, of which 5 were waited for; matrix products, arithmetic and copies ran while one was open for 7% of the time, Pallas kernels for 0%

profile of v1, /device:TPU:1, one launch (start us, length us, event | category | flops | bytes accessed | tf_op | source)
XLA Modules:
  0.0 571.3 jit_solution(12468195734311456578)
XLA Ops:
  11.5 8.6 %all-to-all-start = ((s32[32,1,1]{2,1,0:T(1,128)}), s32[32,1,1]{2,1,0:T(1,128)S(1)}, u32[]{:S(2)}, u32[]{:S(2)}) async-start(s32[32,1,1]{2,1,0:T(1,128)} %copy.77), calls=%async_computation | async-start | bytes 32768 | tf_op jit(solution)/shard_map/all_to_all | solution.py:31
  23.6 5.4 convert_bitcast_fusion.1
  29.0 6.8 %copy.115 = bf16[8,8,128,256]{3,1,2,0:T(8,128)(2,1)} copy(bf16[8,8,128,256]{2,3,1,0:T(8,128)(2,1)} %bitcast.177) | data formatting | bytes 8388608
  43.9 7.5 %all-to-all-start.1 = ((f32[32,1,128,256]{3,2,1,0:T(8,128)}), f32[32,1,128,256]{3,2,1,0:T(8,128)}, u32[]{:S(2)}, u32[]{:S(2)}) async-start(f32[32,1,128,256]{3,2,1,0:T(8,128)} %convolution_bitcast_fusion), calls=%async_computation.1 | async-start | bytes 8388608 | tf_op jit(solution)/shard_map/all_to_all | solution.py:69
  52.7 63.9 %all-to-all-done.1 = f32[32,1,128,256]{3,2,1,0:T(8,128)} async-done(((f32[32,1,128,256]{3,2,1,0:T(8,128)}), f32[32,1,128,256]{3,2,1,0:T(8,128)}, u32[]{:S(2)}, u32[]{:S(2)}) %all-to-all-start.1) | async-done | bytes 4194336 | tf_op jit(solution)/shard_map/all_to_all | solution.py:69
  116.6 4.6 copy.117
  131.3 46.5 %all-gather.5.cloned.1.call-done = bf16[16384,256]{1,0:T(8,128)(2,1)} async-done(((bf16[512,256]{1,0:T(8,128)(2,1)}), bf16[16384,256]{1,0:T(8,128)(2,1)}) %all-gather.5.cloned.1.call-update) | async-done | bytes 8388624 | tf_op jit(solution)/shard_map/all_gather | solution.py:34
  177.8 5.5 gather_fusion
  183.3 4.4 gather_fusion.1
  187.6 5.5 convert_bitcast_fusion.2
  193.1 6.8 %copy.113 = bf16[8,8,128,256]{3,1,2,0:T(8,128)(2,1)} copy(bf16[8,8,128,256]{2,3,1,0:T(8,128)(2,1)} %bitcast.178) | data formatting | bytes 8388608
  206.1 69.7 %all-reduce.7.cloned.1.call-done = (f32[256,512]{0,1:T(8,128)}, f32[256,256]{0,1:T(8,128)}) async-done(((f32[256,512]{0,1:T(8,128)}, f32[256,256]{0,1:T(8,128)}), (f32[256,512]{0,1:T(8,128)}, f32[256,256]{0,1:T(8,128)})) %all-reduce.7.cloned.1.call-update) | async-done | bytes 786448 | tf_op jit(solution)/shard_map/psum | solution.py:87
  278.0 11.7 %cholesky.50 = f32[128,128]{1,0:T(8,128)S(1)} custom-call(f32[128,128]{1,0:T(8,128)S(1)} %cholesky.118), custom_call_target="Cholesky" | custom-call | tf_op jit(solution)/shard_map/jit(cholesky)/cholesky | solution.py:89
  289.8 9.8 %custom-call.18 = f32[1,128,128]{1,2,0:T(8,128)S(1)} custom-call(f32[1,128,128]{2,1,0:T(8,128)S(1)} %get-tuple-element.35), custom_call_target="InvertDiagBlocksLowerTriangular" | custom-call | tf_op jit(solution)/shard_map/jit(cholesky)/cholesky | solution.py:89
  300.1 11.7 %cholesky.105 = f32[128,128]{1,0:T(8,128)S(1)} custom-call(f32[128,128]{1,0:T(8,128)S(1)} %convolution_subtract_fusion.2), custom_call_target="Cholesky" | custom-call | tf_op jit(solution)/shard_map/jit(cholesky)/cholesky | solution.py:89
  313.9 4.2 while.1
  318.1 19.7 %custom-call.19 = f32[2,128,128]{1,2,0:T(8,128)S(1)} custom-call(f32[2,128,128]{2,1,0:T(8,128)S(1)} %get-tuple-element.9), custom_call_target="InvertDiagBlocksLowerTriangular" | custom-call | tf_op jit(solution)/shard_map/jit(_cho_solve)/triangular_solve | solution.py:90
  342.3 66.5 %all-gather.7.cloned.1.call-done = bf16[16384,256]{0,1:T(8,128)(2,1)} async-done(((bf16[512,256]{0,1:T(8,128)(2,1)}), bf16[16384,256]{0,1:T(8,128)(2,1)}) %all-gather.7.cloned.1.call-update) | async-done | bytes 8388624 | tf_op jit(solution)/shard_map/all_gather | solution.py:34
  408.8 12.0 %copy.111 = bf16[16384,256]{1,0:T(8,128)(2,1)} copy(bf16[16384,256]{0,1:T(8,128)(2,1)} %all-gather.7.cloned.1.call-done) | data formatting | bytes 16777216 | tf_op jit(solution)/shard_map/reshape | solution.py:34
  420.7 5.5 gather_fusion.3
  426.2 4.4 gather_fusion.4
  430.6 5.5 convert_bitcast_fusion
  436.0 6.8 %copy.118 = bf16[8,8,128,256]{3,1,2,0:T(8,128)(2,1)} copy(bf16[8,8,128,256]{2,3,1,0:T(8,128)(2,1)} %bitcast.179) | data formatting | bytes 8388608
  447.3 112.9 %all-reduce.5.cloned.1.call-done = f32[2,256,256]{1,2,0:T(8,128)} async-done(((f32[2,256,256]{1,2,0:T(8,128)}), f32[2,256,256]{1,2,0:T(8,128)}) %all-reduce.5.cloned.1.call-update) | async-done | bytes 524304 | tf_op jit(solution)/shard_map/psum | solution.py:105
  (100 shorter events, 53.8 us)
Async XLA Ops:
  7.2 16.4 %copy-start = (bf16[1,1,64,128,128]{4,3,2,1,0:T(8,128)(2,1)S(1)}, bf16[1,1,64,128,128]{4,3,2,1,0:T(8,128)(2,1)}, u32[]{:S(2)}) copy-start(bf16[1,1,64,128,128]{4,3,2,1,0:T(8,128)(2,1)} %param.9) | copy-start | bytes 6291460
  7.2 13.6 %copy-start.1 = (bf16[512,256]{1,0:T(8,128)(2,1)S(1)}, bf16[512,256]{1,0:T(8,128)(2,1)}, u32[]{:S(2)}) copy-start(bf16[512,256]{1,0:T(8,128)(2,1)} %param.14) | copy-start | bytes 786436
  7.2 117.8 %all-gather.9.cloned.1.call-start = ((), (), s32[]{:S(2)}) async-start(), calls=%async_computation.5 | async-start | bytes 8650752 | tf_op jit(solution)/shard_map/all_gather | solution.py:11
  9.4 168.4 %all-gather.5.cloned.1.call-start = ((), (), s32[]{:S(2)}) async-start(), calls=%async_computation.2 | async-start | bytes 8650752 | tf_op jit(solution)/shard_map/all_gather | solution.py:34
  11.5 32.3 %all-to-all-start = ((s32[32,1,1]{2,1,0:T(1,128)}), s32[32,1,1]{2,1,0:T(1,128)S(1)}, u32[]{:S(2)}, u32[]{:S(2)}) async-start(s32[32,1,1]{2,1,0:T(1,128)} %copy.77), calls=%async_computation | async-start | bytes 32768 | tf_op jit(solution)/shard_map/all_to_all | solution.py:31
  29.0 6.8 %copy-start.9 = (s32[1,1,64]{2,1,0:T(1,128)S(1)}, s32[1,1,64]{2,1,0:T(1,128)}, u32[]{:S(2)}) copy-start(s32[1,1,64]{2,1,0:T(1,128)} %param.10) | copy-start | bytes 772
  29.0 6.8 %copy-start.10 = (s32[1,1,64]{2,1,0:T(1,128)S(1)}, s32[1,1,64]{2,1,0:T(1,128)}, u32[]{:S(2)}) copy-start(s32[1,1,64]{2,1,0:T(1,128)} %param.11) | copy-start | bytes 772
  29.0 6.8 %copy-start.12 = (s32[1,1,64]{2,1,0:T(1,128)S(1)}, s32[1,1,64]{2,1,0:T(1,128)}, u32[]{:S(2)}) copy-start(s32[1,1,64]{2,1,0:T(1,128)} %param.12) | copy-start | bytes 772
  39.5 1.1 copy-start.2
  43.9 8.1 %copy-start.11 = (s32[1,1,32,1]{2,3,1,0:T(1,128)S(1)}, s32[1,1,32,1]{2,3,1,0:T(1,128)}, u32[]{:S(2)}) copy-start(s32[1,1,32,1]{2,3,1,0:T(1,128)} %param.13) | copy-start | bytes 388
  43.9 72.7 %all-to-all-start.1 = ((f32[32,1,128,256]{3,2,1,0:T(8,128)}), f32[32,1,128,256]{3,2,1,0:T(8,128)}, u32[]{:S(2)}, u32[]{:S(2)}) async-start(f32[32,1,128,256]{3,2,1,0:T(8,128)} %convolution_bitcast_fusion), calls=%async_computation.1 | async-start | bytes 8388608 | tf_op jit(solution)/shard_map/all_to_all | solution.py:69
  51.4 224.4 %all-reduce.7.cloned.1.call-start = ((), (), s32[]{:S(2)}) async-start(), calls=%async_computation.6 | async-start | bytes 1572864 | tf_op jit(solution)/shard_map/psum | solution.py:87
  199.9 3.2 copy-start.5
  199.9 4.8 copy-start.4
  205.9 202.9 %all-gather.7.cloned.1.call-start = ((), (), s32[]{:S(2)}) async-start(), calls=%async_computation.3 | async-start | bytes 8650752 | tf_op jit(solution)/shard_map/all_gather | solution.py:34
  275.8 61.9 %copy-start.7 = (f32[256,512]{0,1:T(8,128)S(1)}, f32[256,512]{0,1:T(8,128)}, u32[]{:S(2)}) copy-start(f32[256,512]{0,1:T(8,128)} %get-tuple-element.28) | copy-start | bytes 1572868
  341.1 219.1 %all-reduce.5.cloned.1.call-start = ((), (), s32[]{:S(2)}) async-start(), calls=%async_computation.4 | async-start | bytes 1048576 | tf_op jit(solution)/shard_map/psum | solution.py:105
  342.3 103.7 %copy-start.6 = (bf16[512,256]{1,0:T(8,128)(2,1)}, bf16[512,256]{1,0:T(8,128)(2,1)S(1)}, u32[]{:S(2)}) copy-start(bf16[512,256]{1,0:T(8,128)(2,1)S(1)} %copy.90) | copy-start | bytes 786436
  442.9 4.3 copy-start.8
  442.9 117.4 %copy-start.3 = (f32[256,256]{1,0:T(8,128)S(1)}, f32[256,256]{1,0:T(8,128)}, u32[]{:S(2)}) copy-start(f32[256,256]{1,0:T(8,128)} %param.16) | copy-start | bytes 786436
Sparse Core Ops, SparseCore 0:
  11.2 104.7 all-gather.8
  118.5 59.3 all-gather.4
  206.0 69.7 all-reduce.6
  341.3 67.4 all-gather.6
  447.3 112.9 all-reduce.4
